TPU v7x, 512 devices: a whole 4x8x8 slice. The times are simulated.
512 devices in a mesh: language: 8 (over y_hi, core), fsdp: 64 (over y_lo, x, z).
Axes of the slice: x: 4, y: 8 (y_hi: 4, y_lo: 2; y = y_hi * 2 + y_lo), z: 8, core: 2. Of those that a mesh axis runs over, the one named last changes fastest.
Arguments:
- hidden: bfloat16 [16, 8192, 5120], P('language', 'fsdp'), may hold values from -60 to 60
- latent_grad: bfloat16 [16, 8192, 64], P('language', 'fsdp'), may hold values from -0.15625 to 0.15625
- lang_ids: int32 [16], P('language'), may hold values from 0 to 15, each once
- old_weights: float32 [16], replicated, may hold values from 0.02 to 0.2
- param: float32 [5120, 64], P('fsdp'), may hold values from -6 to 6
- first_moment: float32 [5120, 64], P('fsdp'), may hold values from -6 to 6
- second_moment: float32 [5120, 64], P('fsdp'), may hold values from 0.25 to 4
Outputs:
- new_param: float32 [5120, 64], P('fsdp')
- new_first: float32 [5120, 64], P('fsdp')
- new_second: float32 [5120, 64], P('fsdp')
- new_logweights: float32 [16], replicated
Inputs may be any that keep to these rules, and one draw needn't show every extreme that they name: `lang_ids`: each id appears in exactly one slot.
All inputs are finite; a program needn't handle non-finite values.
Results may differ from a plain program's by a relative error of at most 0.0003.
Values may be sent and summed in bfloat16 or wider, within the bound.
A program may use at most 64 MiB of HBM per device.

v0:
```python
import jax
import jax.numpy as jnp
from jax import lax
from jax.sharding import PartitionSpec as P

STEP = 100


def log_weights(by_lang, square, old_weights):
    logits = jnp.log(old_weights) + old_weights.shape[0] * (by_lang / (square + 1e-06))
    return logits - jnp.log(jnp.sum(jnp.exp(logits)))


def local(hidden, latent_grad, lang_ids, old_weights, param, first_moment, second_moment):
    langs = old_weights.shape[0]
    slot_grad = lax.psum_scatter(
        jnp.einsum("ltd,ltr->dlr", hidden, latent_grad, preferred_element_type=jnp.float32),
        "fsdp",
        scatter_dimension=0,
        tiled=True,
    )
    onehot = (lang_ids[:, None] == jnp.arange(langs, dtype=jnp.int32)[None, :]).astype(jnp.float32)
    total = lax.psum(jnp.sum(slot_grad, axis=1), "language")
    dots = jnp.einsum("dlr,dr->l", slot_grad, total, precision=lax.Precision.HIGHEST)
    leader = (lax.axis_index("language") == 0).astype(jnp.float32)
    square_part = jnp.sum(total * total) * leader
    by_lang_part = jnp.dot(dots, onehot, precision=lax.Precision.HIGHEST)
    by_lang, square = lax.psum((by_lang_part, square_part), ("language", "fsdp"))
    new_logweights = log_weights(by_lang, square, old_weights)
    weights = jnp.exp(new_logweights)
    slot_weight = jnp.dot(onehot, weights, precision=lax.Precision.HIGHEST)
    local_update = jnp.einsum("l,dlr->dr", slot_weight, slot_grad, precision=lax.Precision.HIGHEST)
    update = lax.psum(local_update, "language")
    new_first = 0.9 * first_moment + 0.1 * update
    new_second = 0.95 * second_moment + 0.05 * update * update
    first_hat = new_first / (1.0 - 0.9**STEP)
    second_hat = new_second / (1.0 - 0.95**STEP)
    new_param = param - 0.02 * (first_hat / (jnp.sqrt(second_hat) + 1e-08) + 0.1 * param)
    return (new_param, new_first, new_second, new_logweights)


def solution(mesh):
    placed = (
        P("language", "fsdp", None),
        P("language", "fsdp", None),
        P("language"),
        P(),
        P("fsdp", None),
        P("fsdp", None),
        P("fsdp", None),
    )
    return jax.shard_map(
        local,
        mesh=mesh,
        in_specs=placed,
        out_specs=(P("fsdp", None), P("fsdp", None), P("fsdp", None), P()),
        check_vma=False,
    )
```

profile of v0, /device:TPU:1, one launch (start us, length us, event | category | flops | bytes accessed | tf_op | source)
XLA Modules:
  0.0 502.3 jit_solution(7632736756905314304)
XLA Ops:
  7.2 0.0 copy-start
  7.2 0.0 reduce-scatter.4.cloned.1.call-start
  7.2 1.7 copy-done
  8.9 2.8 fusion.7
  11.7 3.2 copy.16
  14.9 0.0 copy-start.5
  14.9 0.0 copy-start.4
  14.9 0.0 copy-start.1
  14.9 0.0 copy-start.2
  14.9 0.0 copy-start.3
  14.9 0.0 reduce-scatter.4.cloned.1.call-update
  15.0 278.8 %reduce-scatter.4.cloned.1.call-done = f32[80,128]{1,0:T(8,128)} async-done(((f32[5120,128]{1,0:T(8,128)}), f32[80,128]{1,0:T(8,128)}) %reduce-scatter.4.cloned.1.call-update) | async-done | bytes 40976
  293.8 0.9 copy.17
  294.7 72.8 %psum.28 = f32[80,64]{0,1:T(8,128)S(1)} all-reduce(f32[80,64]{0,1:T(8,128)S(1)} %reduce_sum.27), channel_id=1, replica_groups=mesh['language'=8,'fsdp'=64] {'language'}, use_global_device_ids=true, to_apply=%region_2.0 | all-reduce | flops 5120 | bytes 40960 | tf_op jit(solution)/shard_map/psum | solution.py:23
  367.5 0.6 multiply_reduce_fusion
  368.1 0.7 convolution_bitcast_fusion.2
  368.7 0.0 copy-done.5
  368.8 0.2 convolution_bitcast_fusion.1
  369.6 97.7 %all-reduce = (f32[16]{0:T(128)S(1)}, f32[]{:T(128)}) all-reduce(f32[16]{0:T(128)S(1)} %convolution_bitcast_fusion.1, f32[]{:T(128)S(6)} %mul.45), channel_id=1, replica_groups=mesh['language'=8,'fsdp'=64] {'language','fsdp'}, use_global_device_ids=true, to_apply=%region_3.0 | all-reduce | flops 17 | bytes 136 | tf_op jit(solution)/shard_map/psum | solution.py:28
  468.0 0.0 copy-done.4
  468.0 0.6 exponential_reduce_fusion
  469.3 0.0 copy-start.6
  469.3 0.2 convolution_bitcast_fusion
  469.5 0.4 fusion
  469.9 24.9 %psum.31 = f32[80,64]{0,1:T(8,128)S(1)} all-reduce(f32[80,64]{0,1:T(8,128)S(1)} %bitcast.34), channel_id=1, replica_groups=mesh['language'=8,'fsdp'=64] {'language'}, use_global_device_ids=true, to_apply=%region_7.0 | all-reduce | flops 5120 | bytes 40960 | tf_op jit(solution)/shard_map/psum | solution.py:33
  494.8 0.0 copy-done.1
  494.8 0.0 copy-done.2
  494.8 0.0 copy-done.3
  494.8 0.7 multiply_subtract_fusion
  495.5 0.0 copy-done.6
  (2 shorter events, 0.0 us)
Async XLA Ops:
  7.2 1.7 copy-start
  7.2 286.6 %reduce-scatter.4.cloned.1.call-start = ((), (), s32[]{:S(2)}) async-start(), calls=%async_computation.1 | async-start | bytes 2662400
  14.9 353.8 %copy-start.5 = (s32[2]{0:T(128)S(1)}, s32[2]{0:T(128)}, u32[]{:S(2)}) copy-start(s32[2]{0:T(128)} %param.9) | copy-start | bytes 28
  14.9 453.0 %copy-start.4 = (f32[16]{0:T(128)S(1)}, f32[16]{0:T(128)}, u32[]{:S(2)}) copy-start(f32[16]{0:T(128)} %param.10) | copy-start | bytes 196
  14.9 479.9 %copy-start.1 = (f32[80,64]{0,1:T(8,128)S(1)}, f32[80,64]{0,1:T(8,128)}, u32[]{:S(2)}) copy-start(f32[80,64]{0,1:T(8,128)} %param.11) | copy-start | bytes 61444
  14.9 479.9 %copy-start.2 = (f32[80,64]{0,1:T(8,128)S(1)}, f32[80,64]{0,1:T(8,128)}, u32[]{:S(2)}) copy-start(f32[80,64]{0,1:T(8,128)} %param.12) | copy-start | bytes 61444
  14.9 479.9 %copy-start.3 = (f32[80,64]{0,1:T(8,128)S(1)}, f32[80,64]{0,1:T(8,128)}, u32[]{:S(2)}) copy-start(f32[80,64]{0,1:T(8,128)} %param.13) | copy-start | bytes 61444
  469.3 26.2 %copy-start.6 = (f32[16]{0:T(128)}, f32[16]{0:T(128)S(1)}, u32[]{:S(2)}) copy-start(f32[16]{0:T(128)S(1)} %broadcast_subtract_fusion) | copy-start | bytes 196
Sparse Core Ops, SparseCore 0:
  15.1 278.6 reduce-scatter.3
where the time goes:
time: 506 us; the launch traced here: 502 us
  waiting for transfers between devices  279 us (55%)
  blocking collectives  195 us (39%)
  between operations  16.1 us (3%)
  local copies, waits for them, and re-layouts  5.81 us (1%)
    unnamed x2, waiting for transfers between devices  279 us
    psum x1, blocking collectives, local(): lax.psum((by_lang_part, square_part), ('language', 'fsdp'))  97.7 us
    psum x1, blocking collectives, local(): total = lax.psum(jnp.sum(slot_grad, axis=1), 'language')  72.8 us
    psum x1, blocking collectives, local(): update = lax.psum(local_update, 'language')  24.9 us
  transfers between devices with their start and end apart: 1, of which 1 were waited for; matrix products, arithmetic and copies ran while one was open for 0% of the time, Pallas kernels for 0%

commit v1 on v0

v1 whole, which is shorter than its diff:
```python
import functools

import jax
import jax.numpy as jnp
from jax import lax
from jax.experimental import pallas as pl
from jax.experimental.pallas import tpu as pltpu
from jax.sharding import PartitionSpec as P

STEP = 100
GRID = {64: (2, 4, 8), 8: (2, 2, 2)}
RY, RX, RZ = 32, 32, 16
F32 = jnp.float32
WIRE = jnp.float32


def kernel(
    nl, ny, nx, nz,
    hid, lat, ids, old, param, first, second,
    new_param, new_first, new_second, new_logw,
    hv, ys, xs, zs, yr, xr, zr, y2s, x2s, z2s, y2r, x2r, z2r, y3s, x3s, z3s, y3r, x3r, z3r,
    gath, oh, ar1, ar2,
    hsem, ysend, yrecv, xsend, xrecv, zsend, zrecv,
    y2send, y2recv, x2send, x2recv, z2send, z2recv,
    y3send, y3recv, x3send, x3recv, z3send, z3recv,
    gsend, grecv, osend, orecv, a1send, a1recv, a2send, a2recv,
):
    g = lax.axis_index("language")
    f = lax.axis_index("fsdp")
    y = f // (nx * nz)
    x = (f // nz) % nx
    z = f % nz
    ranks = lat.shape[1]
    toks = hid.shape[1]
    cols = 2 * ranks
    blk = hid.shape[2] // (ny * nx)

    def at(yy, xx, zz):
        return {"fsdp": (yy * nx + xx) * nz + zz, "language": g}

    def lang(gg):
        return {"fsdp": f, "language": gg}

    def hop(v, d, n):
        return lax.rem(v + d, n)

    zpeers = [at(y, x, hop(z, d, nz)) for d in range(1, nz)]
    xpeers = [at(y, hop(x, d, nx), z) for d in range(1, nx)]
    ypeer = at(1 - y, x, z)
    diag = [at(1 - y, hop(x, d, nx), z) for d in range(1, nx)]
    lpeers = [lang(hop(g, d, nl)) for d in range(1, nl)]
    peers = [ypeer] + xpeers + zpeers + lpeers + diag

    barrier = pltpu.get_barrier_semaphore()
    for p in peers:
        pl.semaphore_signal(barrier, inc=1, device_id=p, device_id_type=pl.DeviceIdType.MESH)

    def send(src, dst, ssem, rsem, dev):
        c = pltpu.make_async_remote_copy(
            src_ref=src, dst_ref=dst, send_sem=ssem, recv_sem=rsem,
            device_id=dev, device_id_type=pl.DeviceIdType.MESH,
        )
        c.start()
        sent.append(c)

    def wait(dst, rsem):
        pltpu.make_async_copy(dst, dst, rsem).wait()

    sent = []
    xorder = [2, 1, 3, 0] if nx == 4 else list(range(1, nx)) + [0]
    order = [(dy, dx) for dy in (1, 0) for dx in xorder]
    loads = []
    for i, (dy, dx) in enumerate(order):
        c = hop(y, dy, ny) * nx + hop(x, dx, nx)
        at0 = c * blk
        if blk % 128 == 0:
            at0 = pl.multiple_of(at0, 128)
        cp = pltpu.make_async_copy(hid.at[:, :, pl.ds(at0, blk)], hv.at[i], hsem.at[i])
        cp.start()
        loads.append(cp)

    lane = lax.broadcasted_iota(jnp.int32, (1, 128), 1)
    row = lax.broadcasted_iota(jnp.int32, (2, 128), 0)
    lane2 = lax.broadcasted_iota(jnp.int32, (2, 128), 1)
    mine = jnp.where(row == 0, ids[0], ids[1])
    oh[g] = (mine == lane2).astype(F32)
    weights_old = jnp.ones((1, 128), F32)
    for k in range(old.shape[0]):
        weights_old = jnp.where(lane == k, old[k], weights_old)

    zero = jnp.zeros((ranks, toks), jnp.bfloat16)
    lhs = jnp.concatenate(
        [jnp.concatenate([lat[0], zero], axis=1), jnp.concatenate([zero, lat[1]], axis=1)], axis=0
    )

    for i, (dy, dx) in enumerate(order):
        yy, xx = hop(y, dy, ny), hop(x, dx, nx)
        loads[i].wait()
        rhs = hv[i].reshape(2 * toks, blk)
        part = jnp.dot(lhs, rhs, preferred_element_type=F32)
        part = part.T.reshape(nz, RY + RX + RZ, cols).astype(WIRE)
        ys[yy, xx] = part[:, :RY]
        xs[xx, yy] = part[:, RY : RY + RX]
        zs[:, yy, xx] = part[:, RY + RX :]
        if i == 0:
            pl.semaphore_wait(barrier, len(peers))
        if dy:
            send(ys.at[yy, xx], yr.at[xx], ysend.at[dx], yrecv.at[dx], ypeer)
        if dx:
            send(xs.at[xx, yy], xr.at[dx - 1, yy], xsend.at[dx - 1, dy], xrecv.at[dx - 1, dy], xpeers[dx - 1])
    for d in range(1, nz):
        send(zs.at[hop(z, d, nz)], zr.at[d - 1], zsend.at[d - 1], zrecv.at[d - 1], zpeers[d - 1])
    for d in range(1, nl):
        send(oh.at[g], oh.at[g], osend.at[d - 1], orecv.at[d - 1], lpeers[d - 1])

    for dx in xorder:
        xx = hop(x, dx, nx)
        wait(yr.at[xx], yrecv.at[dx])
        y2s[xx] = (ys[y, xx].astype(F32) + yr[xx].astype(F32)).astype(WIRE)
        if dx:
            send(y2s.at[xx], y2r.at[dx - 1], y2send.at[dx - 1], y2recv.at[dx - 1], xpeers[dx - 1])
    for dy in (1, 0):
        yy = hop(y, dy, ny)
        acc = xs[x, yy].astype(F32)
        for d in range(1, nx):
            wait(xr.at[d - 1, yy], xrecv.at[d - 1, dy])
            acc = acc + xr[d - 1, yy].astype(F32)
        x2s[yy] = acc.astype(WIRE)
        if dy:
            send(x2s.at[yy], x2r, x2send, x2recv, ypeer)
    acc = zs[z].astype(F32)
    for d in range(1, nz):
        wait(zr.at[d - 1], zrecv.at[d - 1])
        acc = acc + zr[d - 1].astype(F32)
    z2s[...] = acc.astype(WIRE)
    send(z2s.at[1 - y], z2r, z2send, z2recv, ypeer)

    wait(x2r, x2recv)
    x3s[...] = (x2s[y].astype(F32) + x2r[...].astype(F32)).astype(WIRE)
    for d in range(1, nz):
        send(x3s.at[hop(z, d, nz)], x3r.at[d - 1], x3send.at[d - 1], x3recv.at[d - 1], zpeers[d - 1])
    acc = y2s[x].astype(F32)
    for d in range(1, nx):
        wait(y2r.at[d - 1], y2recv.at[d - 1])
        acc = acc + y2r[d - 1].astype(F32)
    y3s[...] = acc.astype(WIRE)
    for d in range(1, nz):
        send(y3s.at[hop(z, d, nz)], y3r.at[d - 1], y3send.at[d - 1], y3recv.at[d - 1], zpeers[d - 1])
    wait(z2r, z2recv)
    z3s[...] = (z2s[y].astype(F32) + z2r[...].astype(F32)).astype(WIRE)
    for d in range(1, nx):
        send(z3s.at[hop(x, d, nx)], z3r.at[d - 1], z3send.at[d - 1], z3recv.at[d - 1], xpeers[d - 1])

    parts = ((0, RY), (RY, RX), (RY + RX, RZ))

    def finish(own, r, rsem, n, part):
        lo, size = parts[part]
        acc = own.astype(F32)
        for d in range(1, n):
            wait(r.at[d - 1], rsem.at[d - 1])
            acc = acc + r[d - 1].astype(F32)
        gath[g, lo : lo + size] = acc.astype(WIRE)
        for d in range(1, nl):
            ref = gath.at[g, pl.ds(lo, size)]
            send(ref, ref, gsend.at[part, d - 1], grecv.at[part, d - 1], lpeers[d - 1])

    finish(x3s[z], x3r, x3recv, nz, 1)
    finish(z3s[x], z3r, z3recv, nx, 2)
    finish(y3s[z], y3r, y3recv, nz, 0)

    for d in range(1, nl):
        src = hop(g, nl - d, nl)
        wait(oh.at[src], orecv.at[d - 1])
        for part, (lo, size) in enumerate(parts):
            wait(gath.at[src, pl.ds(lo, size)], grecv.at[part, d - 1])

    slots = gath[...].astype(F32)
    total = jnp.sum(slots, axis=0)
    both = total + pltpu.roll(total, ranks, 1)
    prods = jnp.sum(slots * both[None], axis=1)
    first_slot = lane < ranks
    dot0 = jnp.sum(jnp.where(first_slot, prods, 0.0), axis=1, keepdims=True)
    dot1 = jnp.sum(jnp.where(first_slot, 0.0, prods), axis=1, keepdims=True)
    square = jnp.sum(jnp.where(first_slot, jnp.sum(both * both, axis=0, keepdims=True), 0.0), axis=1, keepdims=True)
    oh0, oh1 = oh[:, 0, :], oh[:, 1, :]
    vec = jnp.sum(oh0 * dot0 + oh1 * dot1, axis=0, keepdims=True)
    langs = old.shape[0]
    vec = jnp.where(lane == langs, square, vec)

    ar1[z] = vec
    for d in range(1, nz):
        send(ar1.at[z], ar1.at[z], a1send.at[d - 1], a1recv.at[d - 1], zpeers[d - 1])
    for d in range(1, nz):
        wait(ar1.at[hop(z, nz - d, nz)], a1recv.at[d - 1])
    vec = jnp.sum(ar1[...], axis=0)
    me = y * nx + x
    ar2[me] = vec
    for dy in range(ny):
        for dx in range(nx):
            j = dy * nx + dx
            if j:
                dev = xpeers[dx - 1] if dy == 0 else (diag[dx - 1] if dx else ypeer)
                send(ar2.at[me], ar2.at[me], a2send.at[j - 1], a2recv.at[j - 1], dev)
    for dy in range(ny):
        for dx in range(nx):
            j = dy * nx + dx
            if j:
                src = hop(y, ny - dy, ny) * nx + hop(x, nx - dx, nx)
                wait(ar2.at[src], a2recv.at[j - 1])
    vec = jnp.sum(ar2[...], axis=0)

    square = jnp.sum(jnp.where(lane == langs, vec, 0.0), axis=1, keepdims=True) + 1e-06
    valid = lane < langs
    logits = jnp.log(weights_old) + langs * (jnp.where(valid, vec, 0.0) / square)
    norm = jnp.log(jnp.sum(jnp.where(valid, jnp.exp(logits), 0.0), axis=1, keepdims=True))
    logw = logits - norm
    new_logw[...] = logw
    weights = jnp.where(valid, jnp.exp(logw), 0.0)
    w0 = jnp.sum(oh0 * weights, axis=1, keepdims=True)
    w1 = jnp.sum(oh1 * weights, axis=1, keepdims=True)
    slot_weight = jnp.where(first_slot, w0, w1)
    update = jnp.sum(slots * slot_weight[:, None, :], axis=0).T
    update = update[:ranks] + update[ranks:]
    m = 0.9 * first[...] + 0.1 * update
    v = 0.95 * second[...] + 0.05 * update * update
    new_first[...] = m
    new_second[...] = v
    m_hat = m / (1.0 - 0.9**STEP)
    v_hat = v / (1.0 - 0.95**STEP)
    p = param[...]
    new_param[...] = p - 0.02 * (m_hat / (jnp.sqrt(v_hat) + 1e-08) + 0.1 * p)

    for c in sent:
        c.wait_send()


def local(nl, ny, nx, nz, hidden, latent_grad, lang_ids, old_weights, param, first_moment, second_moment):
    rows, ranks = param.shape
    cols = 2 * ranks
    assert rows == RY + RX + RZ and hidden.shape[0] == 2
    blk = hidden.shape[2] // (ny * nx)
    vmem = pl.BlockSpec(memory_space=pltpu.VMEM)
    smem = pl.BlockSpec(memory_space=pltpu.SMEM)
    dma = pltpu.SemaphoreType.DMA
    b = lambda *s: pltpu.VMEM(s + (cols,), WIRE)
    mat = jax.ShapeDtypeStruct((ranks, rows), F32)
    scratch = [
        pltpu.VMEM((ny * nx, 2, hidden.shape[1], blk), jnp.bfloat16),
        b(ny, nx, nz, RY), b(nx, ny, nz, RX), b(nz, ny, nx, RZ),
        b(nx, nz, RY), b(nx - 1, ny, nz, RX), b(nz - 1, ny, nx, RZ),
        b(nx, nz, RY), b(ny, nz, RX), b(ny, nx, RZ),
        b(nx - 1, nz, RY), b(nz, RX), b(nx, RZ),
        b(nz, RY), b(nz, RX), b(nx, RZ),
        b(nz - 1, RY), b(nz - 1, RX), b(nx - 1, RZ),
        b(nl, rows),
        pltpu.VMEM((nl, 2, 128), F32),
        pltpu.VMEM((nz, 1, 128), F32),
        pltpu.VMEM((ny * nx, 1, 128), F32),
        dma((ny * nx,)),
        dma((nx,)), dma((nx,)), dma((nx - 1, ny)), dma((nx - 1, ny)), dma((nz - 1,)), dma((nz - 1,)),
        dma((nx - 1,)), dma((nx - 1,)), dma, dma, dma, dma,
        dma((nz - 1,)), dma((nz - 1,)), dma((nz - 1,)), dma((nz - 1,)), dma((nx - 1,)), dma((nx - 1,)),
        dma((3, nl - 1)), dma((3, nl - 1)), dma((nl - 1,)), dma((nl - 1,)),
        dma((nz - 1,)), dma((nz - 1,)), dma((ny * nx - 1,)), dma((ny * nx - 1,)),
    ]
    outs = pl.pallas_call(
        functools.partial(kernel, nl, ny, nx, nz),
        out_shape=(mat, mat, mat, jax.ShapeDtypeStruct((1, 128), F32)),
        in_specs=[pl.BlockSpec(memory_space=pl.ANY), vmem, smem, smem, vmem, vmem, vmem],
        out_specs=(vmem, vmem, vmem, vmem),
        scratch_shapes=scratch,
        compiler_params=pltpu.CompilerParams(
            collective_id=0, has_side_effects=True, vmem_limit_bytes=61 * 1024 * 1024
        ),
        name="reweighted_step",
    )(
        hidden, latent_grad.transpose(0, 2, 1), lang_ids, old_weights,
        param.T, first_moment.T, second_moment.T,
    )
    return (outs[0].T, outs[1].T, outs[2].T, outs[3][0, : old_weights.shape[0]])


def solution(mesh):
    nl = mesh.shape["language"]
    ny, nx, nz = GRID[mesh.shape["fsdp"]]
    placed = (
        P("language", "fsdp", None),
        P("language", "fsdp", None),
        P("language"),
        P(),
        P("fsdp", None),
        P("fsdp", None),
        P("fsdp", None),
    )
    return jax.shard_map(
        functools.partial(local, nl, ny, nx, nz),
        mesh=mesh,
        in_specs=placed,
        out_specs=(P("fsdp", None), P("fsdp", None), P("fsdp", None), P()),
        check_vma=False,
    )
```

time: 506 us -> 64.5 us (0.13)
  waiting for transfers between devices: 279 us -> 0 us
  blocking collectives: 195 us -> 0 us
  Pallas kernels: 0 us -> 57.4 us
  between operations: 16.1 us -> 0.64 us
    unnamed x2 -> x0, waiting for transfers between devices: 279 us -> none
    psum x3 -> x0, blocking collectives: 195 us -> none  [the longest x1 97.7 us: local(): lax.psum((by_lang_part, square_part), ('language', 'fsdp'))]
    pallas_call x0 -> x1, Pallas kernels: none -> 57.4 us  [local(): pl.pallas_call(functools.partial(kernel, nl, ny, nx, nz), out_shape=(mat,...]
  transfers between devices with their start and end apart: 1 -> 0, of which waited for: 1 -> 0; matrix products, arithmetic and copies ran while one was open for 0% -> 0% of each run, Pallas kernels for 0% -> 0%
where the time goes in v1:
time: 64.5 us; the launch traced here: 63.3 us
  Pallas kernels  57.4 us (89%)
  local copies, waits for them, and re-layouts  5.31 us (8%)
    pallas_call x1, Pallas kernels, local(): pl.pallas_call(functools.partial(kernel, nl, ny, nx, nz), out_shape=(mat,...  57.4 us
    unnamed x3, local copies, waits for them, and re-layouts  4.12 us

profile of v1, /device:TPU:1, one launch (start us, length us, event | category | flops | bytes accessed | tf_op | source)
XLA Modules:
  0.0 63.3 jit_solution(3809763247149196329)
XLA Ops:
  0.6 57.4 %reweighted_step.1 = (f32[64,80]{1,0:T(8,128)}, f32[64,80]{1,0:T(8,128)}, f32[64,80]{1,0:T(8,128)}, f32[1,128]{1,0:T(1,128)}) custom-call(bf16[2,128,5120]{2,1,0:T(8,128)(2,1)} %hid.1, bf16[2,64,128]{2,1,0:T(8,128)(2,1)} %bitcast.9, s32[2]{0:T(128)} %ids.1, f32[16]{0:T(128)} %old.1, f32[64,80]{1,0:T(8,128)} %bitcast.10, f32[64,80]{1,0:T(8,128)} %bitcast.11, ...), custom_call_target="tpu_custom_call" | custom-call | tf_op jit(solution)/shard_map/reweighted_step/pallas_call | solution.py:266
  58.0 1.2 %slice_bitcast_fusion = f32[16]{0:T(128)} fusion(f32[1,128]{1,0:T(1,128)} %get-tuple-element.11), kind=kLoop, calls=%fused_computation | loop fusion | bytes 128 | tf_op jit(solution)/shard_map/squeeze | solution.py:280
  59.2 1.4 %copy.14 = f32[80,64]{0,1:T(8,128)} copy(f32[80,64]{0,1:T(8,128)} %bitcast.15) | data formatting | bytes 40960
  60.6 1.4 %copy.15 = f32[80,64]{0,1:T(8,128)} copy(f32[80,64]{0,1:T(8,128)} %bitcast.14) | data formatting | bytes 40960
  62.0 1.4 %copy.16 = f32[80,64]{0,1:T(8,128)} copy(f32[80,64]{0,1:T(8,128)} %bitcast.13) | data formatting | bytes 40960

commit v2 on v1

--- a/solution.py
+++ b/solution.py
@@ -12,18 +12,19 @@
 RY, RX, RZ = 32, 32, 16
 F32 = jnp.float32
 WIRE = jnp.float32
+BF16 = jnp.bfloat16
 
 
 def kernel(
     nl, ny, nx, nz,
-    hid, lat, ids, old, param, first, second,
-    new_param, new_first, new_second, new_logw,
+    hid, lat, ids, old,
+    update, new_logw,
     hv, ys, xs, zs, yr, xr, zr, y2s, x2s, z2s, y2r, x2r, z2r, y3s, x3s, z3s, y3r, x3r, z3r,
-    gath, oh, ar1, ar2,
+    high, low, oh, ar,
     hsem, ysend, yrecv, xsend, xrecv, zsend, zrecv,
     y2send, y2recv, x2send, x2recv, z2send, z2recv,
     y3send, y3recv, x3send, x3recv, z3send, z3recv,
-    gsend, grecv, osend, orecv, a1send, a1recv, a2send, a2recv,
+    gsend, grecv, lsend, lrecv, osend, orecv, asend, arecv,
 ):
     g = lax.axis_index("language")
     f = lax.axis_index("fsdp")
@@ -47,21 +48,21 @@
     zpeers = [at(y, x, hop(z, d, nz)) for d in range(1, nz)]
     xpeers = [at(y, hop(x, d, nx), z) for d in range(1, nx)]
     ypeer = at(1 - y, x, z)
-    diag = [at(1 - y, hop(x, d, nx), z) for d in range(1, nx)]
     lpeers = [lang(hop(g, d, nl)) for d in range(1, nl)]
-    peers = [ypeer] + xpeers + zpeers + lpeers + diag
+    peers = [ypeer] + xpeers + zpeers + lpeers
 
     barrier = pltpu.get_barrier_semaphore()
     for p in peers:
         pl.semaphore_signal(barrier, inc=1, device_id=p, device_id_type=pl.DeviceIdType.MESH)
 
-    def send(src, dst, ssem, rsem, dev):
+    def send(src, dst, ssem, rsem, dev, keep=True):
         c = pltpu.make_async_remote_copy(
             src_ref=src, dst_ref=dst, send_sem=ssem, recv_sem=rsem,
             device_id=dev, device_id_type=pl.DeviceIdType.MESH,
         )
         c.start()
-        sent.append(c)
+        if keep:
+            sent.append(c)
 
     def wait(dst, rsem):
         pltpu.make_async_copy(dst, dst, rsem).wait()
@@ -159,22 +160,26 @@
         for d in range(1, n):
             wait(r.at[d - 1], rsem.at[d - 1])
             acc = acc + r[d - 1].astype(F32)
-        gath[g, lo : lo + size] = acc.astype(WIRE)
+        top = acc.astype(BF16)
+        high[g, lo : lo + size] = top
+        low[g, lo : lo + size] = (acc - top.astype(F32)).astype(BF16)
         for d in range(1, nl):
-            ref = gath.at[g, pl.ds(lo, size)]
+            ref = high.at[g, pl.ds(lo, size)]
             send(ref, ref, gsend.at[part, d - 1], grecv.at[part, d - 1], lpeers[d - 1])
 
     finish(x3s[z], x3r, x3recv, nz, 1)
     finish(z3s[x], z3r, z3recv, nx, 2)
     finish(y3s[z], y3r, y3recv, nz, 0)
+    for d in range(1, nl):
+        send(low.at[g], low.at[g], lsend.at[d - 1], lrecv.at[d - 1], lpeers[d - 1])
 
     for d in range(1, nl):
         src = hop(g, nl - d, nl)
         wait(oh.at[src], orecv.at[d - 1])
         for part, (lo, size) in enumerate(parts):
-            wait(gath.at[src, pl.ds(lo, size)], grecv.at[part, d - 1])
-
-    slots = gath[...].astype(F32)
+            wait(high.at[src, pl.ds(lo, size)], grecv.at[part, d - 1])
+
+    slots = high[...].astype(F32)
     total = jnp.sum(slots, axis=0)
     both = total + pltpu.roll(total, ranks, 1)
     prods = jnp.sum(slots * both[None], axis=1)
@@ -187,27 +192,13 @@
     langs = old.shape[0]
     vec = jnp.where(lane == langs, square, vec)
 
-    ar1[z] = vec
-    for d in range(1, nz):
-        send(ar1.at[z], ar1.at[z], a1send.at[d - 1], a1recv.at[d - 1], zpeers[d - 1])
-    for d in range(1, nz):
-        wait(ar1.at[hop(z, nz - d, nz)], a1recv.at[d - 1])
-    vec = jnp.sum(ar1[...], axis=0)
-    me = y * nx + x
-    ar2[me] = vec
-    for dy in range(ny):
-        for dx in range(nx):
-            j = dy * nx + dx
-            if j:
-                dev = xpeers[dx - 1] if dy == 0 else (diag[dx - 1] if dx else ypeer)
-                send(ar2.at[me], ar2.at[me], a2send.at[j - 1], a2recv.at[j - 1], dev)
-    for dy in range(ny):
-        for dx in range(nx):
-            j = dy * nx + dx
-            if j:
-                src = hop(y, ny - dy, ny) * nx + hop(x, nx - dx, nx)
-                wait(ar2.at[src], a2recv.at[j - 1])
-    vec = jnp.sum(ar2[...], axis=0)
+    ar[f] = vec
+    n = ny * nx * nz
+    for d in range(1, n):
+        yy, xx, zz = hop(y, d // (nx * nz), ny), hop(x, d // nz % nx, nx), hop(z, d % nz, nz)
+        send(ar.at[f], ar.at[f], asend, arecv, at(yy, xx, zz), False)
+    wait(ar.at[pl.ds(0, n - 1)], arecv)
+    vec = jnp.sum(ar[...], axis=0)
 
     square = jnp.sum(jnp.where(lane == langs, vec, 0.0), axis=1, keepdims=True) + 1e-06
     valid = lane < langs
@@ -219,8 +210,19 @@
     w0 = jnp.sum(oh0 * weights, axis=1, keepdims=True)
     w1 = jnp.sum(oh1 * weights, axis=1, keepdims=True)
     slot_weight = jnp.where(first_slot, w0, w1)
-    update = jnp.sum(slots * slot_weight[:, None, :], axis=0).T
-    update = update[:ranks] + update[ranks:]
+    for d in range(1, nl):
+        wait(low.at[hop(g, nl - d, nl)], lrecv.at[d - 1])
+    slots = slots + low[...].astype(F32)
+    total = jnp.sum(slots * slot_weight[:, None, :], axis=0).T
+    update[...] = total[:ranks] + total[ranks:]
+
+    for c in sent:
+        c.wait_send()
+    pltpu.make_async_copy(ar.at[pl.ds(0, n - 1)], ar.at[pl.ds(0, n - 1)], asend).wait()
+
+
+def adamw(grad, logw, param, first, second, new_param, new_first, new_second, new_logw):
+    update = grad[...]
     m = 0.9 * first[...] + 0.1 * update
     v = 0.95 * second[...] + 0.05 * update * update
     new_first[...] = m
@@ -229,9 +231,7 @@
     v_hat = v / (1.0 - 0.95**STEP)
     p = param[...]
     new_param[...] = p - 0.02 * (m_hat / (jnp.sqrt(v_hat) + 1e-08) + 0.1 * p)
-
-    for c in sent:
-        c.wait_send()
+    new_logw[...] = logw[0, : new_logw.shape[0]]
 
 
 def local(nl, ny, nx, nz, hidden, latent_grad, lang_ids, old_weights, param, first_moment, second_moment):
@@ -252,32 +252,35 @@
         b(nx - 1, nz, RY), b(nz, RX), b(nx, RZ),
         b(nz, RY), b(nz, RX), b(nx, RZ),
         b(nz - 1, RY), b(nz - 1, RX), b(nx - 1, RZ),
-        b(nl, rows),
+        pltpu.VMEM((nl, rows, cols), BF16), pltpu.VMEM((nl, rows, cols), BF16),
         pltpu.VMEM((nl, 2, 128), F32),
-        pltpu.VMEM((nz, 1, 128), F32),
-        pltpu.VMEM((ny * nx, 1, 128), F32),
+        pltpu.VMEM((ny * nx * nz, 1, 128), F32),
         dma((ny * nx,)),
         dma((nx,)), dma((nx,)), dma((nx - 1, ny)), dma((nx - 1, ny)), dma((nz - 1,)), dma((nz - 1,)),
         dma((nx - 1,)), dma((nx - 1,)), dma, dma, dma, dma,
         dma((nz - 1,)), dma((nz - 1,)), dma((nz - 1,)), dma((nz - 1,)), dma((nx - 1,)), dma((nx - 1,)),
         dma((3, nl - 1)), dma((3, nl - 1)), dma((nl - 1,)), dma((nl - 1,)),
-        dma((nz - 1,)), dma((nz - 1,)), dma((ny * nx - 1,)), dma((ny * nx - 1,)),
+        dma((nl - 1,)), dma((nl - 1,)), dma, dma,
     ]
-    outs = pl.pallas_call(
+    update, logw = pl.pallas_call(
         functools.partial(kernel, nl, ny, nx, nz),
-        out_shape=(mat, mat, mat, jax.ShapeDtypeStruct((1, 128), F32)),
-        in_specs=[pl.BlockSpec(memory_space=pl.ANY), vmem, smem, smem, vmem, vmem, vmem],
-        out_specs=(vmem, vmem, vmem, vmem),
+        out_shape=(mat, jax.ShapeDtypeStruct((1, 128), F32)),
+        in_specs=[pl.BlockSpec(memory_space=pl.ANY), vmem, smem, smem],
+        out_specs=(vmem, vmem),
         scratch_shapes=scratch,
         compiler_params=pltpu.CompilerParams(
             collective_id=0, has_side_effects=True, vmem_limit_bytes=61 * 1024 * 1024
         ),
-        name="reweighted_step",
-    )(
-        hidden, latent_grad.transpose(0, 2, 1), lang_ids, old_weights,
-        param.T, first_moment.T, second_moment.T,
-    )
-    return (outs[0].T, outs[1].T, outs[2].T, outs[3][0, : old_weights.shape[0]])
+        name="reweight",
+    )(hidden, latent_grad.transpose(0, 2, 1), lang_ids, old_weights)
+    outs = pl.pallas_call(
+        adamw,
+        out_shape=(mat, mat, mat, jax.ShapeDtypeStruct(old_weights.shape, F32)),
+        in_specs=[vmem] * 5,
+        out_specs=(vmem,) * 4,
+        name="adamw",
+    )(update, logw, param.T, first_moment.T, second_moment.T)
+    return (outs[0].T, outs[1].T, outs[2].T, outs[3])
 
 
 def solution(mesh):

time: 64.5 us -> 58.2 us (0.902); the launches traced: 63.3 us -> 58 us
  local copies, waits for them, and re-layouts: 5.31 us -> 0 us
    unnamed x3 -> x0, local copies, waits for them, and re-layouts: 4.12 us -> none
    pallas_call x1, Pallas kernels: 57.4 us -> 55.9 us  [local(): pl.pallas_call(functools.partial(kernel, nl, ny, nx, nz), out_shape=(mat,...]
    pallas_call x0 -> x1, Pallas kernels: none -> 1.47 us  [local(): pl.pallas_call(adamw, out_shape=(mat, mat, mat, jax.ShapeDtypeStruct(old_...]
    squeeze x1 -> x0, local copies, waits for them, and re-layouts: 1.19 us -> none  [local(): return (outs[0].T, outs[1].T, outs[2].T, outs[3][0, :old_weights.shape[0]])]
where the time goes in v2:
time: 58.2 us; the launch traced here: 58 us
  Pallas kernels  57.3 us (98%)
  between operations  0.64 us (1%)
    pallas_call x1, Pallas kernels, local(): pl.pallas_call(functools.partial(kernel, nl, ny, nx, nz), out_shape=(mat,...  55.9 us
    pallas_call x1, Pallas kernels, local(): pl.pallas_call(adamw, out_shape=(mat, mat, mat, jax.ShapeDtypeStruct(old_...  1.47 us

profile of v2, /device:TPU:1, one launch (start us, length us, event | category | flops | bytes accessed | tf_op | source)
XLA Modules:
  0.0 58.0 jit_solution(56456477929993360)
XLA Ops:
  0.6 55.9 %reweight.1 = (f32[64,80]{1,0:T(8,128)}, f32[1,128]{1,0:T(1,128)}) custom-call(bf16[2,128,5120]{2,1,0:T(8,128)(2,1)} %hid.1, bf16[2,64,128]{2,1,0:T(8,128)(2,1)} %bitcast.7, s32[2]{0:T(128)} %ids.1, f32[16]{0:T(128)} %old.1), custom_call_target="tpu_custom_call" | custom-call | tf_op jit(solution)/shard_map/reweight/pallas_call | solution.py:265
  56.5 1.5 %adamw.1 = (f32[64,80]{1,0:T(8,128)}, f32[64,80]{1,0:T(8,128)}, f32[64,80]{1,0:T(8,128)}, f32[16]{0:T(128)}) custom-call(f32[64,80]{1,0:T(8,128)} %get-tuple-element.10.grad, f32[1,128]{1,0:T(1,128)} %get-tuple-element.11.logw, f32[64,80]{1,0:T(8,128)} %bitcast.8, f32[64,80]{1,0:T(8,128)} %bitcast.9, f32[64,80]{1,0:T(8,128)} %bitcast.10), custom_call_target="tpu_custom_call" | custom-call | tf_op jit(solution)/shard_map/adamw/pallas_call | solution.py:276

commit v3 on v2

--- a/solution.py
+++ b/solution.py
@@ -11,8 +11,8 @@
 GRID = {64: (2, 4, 8), 8: (2, 2, 2)}
 RY, RX, RZ = 32, 32, 16
 F32 = jnp.float32
-WIRE = jnp.float32
 BF16 = jnp.bfloat16
+ORDER = ((1, 0), (2, 0), (1, 1), (3, 0), (2, 1), (3, 1))
 
 
 def kernel(
@@ -20,7 +20,7 @@
     hid, lat, ids, old,
     update, new_logw,
     hv, ys, xs, zs, yr, xr, zr, y2s, x2s, z2s, y2r, x2r, z2r, y3s, x3s, z3s, y3r, x3r, z3r,
-    high, low, oh, ar,
+    both, oh, ar,
     hsem, ysend, yrecv, xsend, xrecv, zsend, zrecv,
     y2send, y2recv, x2send, x2recv, z2send, z2recv,
     y3send, y3recv, x3send, x3recv, z3send, z3recv,
@@ -94,99 +94,124 @@
         [jnp.concatenate([lat[0], zero], axis=1), jnp.concatenate([zero, lat[1]], axis=1)], axis=0
     )
 
+    def split(value):
+        high = value.astype(BF16)
+        return high, (value - high.astype(F32)).astype(BF16)
+
+    def put(k, dst, terms):
+        total = terms[0].astype(F32)
+        for term in terms[1:]:
+            total = total + term.astype(F32)
+        if k == 0:
+            dst(0)[...], dst(1)[...] = split(total)
+        else:
+            dst(1)[...] = (total + dst(1)[...].astype(F32)).astype(BF16)
+
+    def first_sends(k, dy, dx):
+        yy, xx = hop(y, dy, ny), hop(x, dx, nx)
+        if dy:
+            send(ys.at[k, yy, xx], yr.at[k, xx], ysend.at[k, dx], yrecv.at[k, dx], ypeer)
+        if dx:
+            send(
+                xs.at[k, xx, yy], xr.at[k, dx - 1, yy], xsend.at[k, dx - 1, dy], xrecv.at[k, dx - 1, dy],
+                xpeers[dx - 1],
+            )
+
+    def last_sends(k):
+        for d in range(1, nz):
+            send(zs.at[k, hop(z, d, nz)], zr.at[k, d - 1], zsend.at[k, d - 1], zrecv.at[k, d - 1], zpeers[d - 1])
+
     for i, (dy, dx) in enumerate(order):
         yy, xx = hop(y, dy, ny), hop(x, dx, nx)
         loads[i].wait()
         rhs = hv[i].reshape(2 * toks, blk)
         part = jnp.dot(lhs, rhs, preferred_element_type=F32)
-        part = part.T.reshape(nz, RY + RX + RZ, cols).astype(WIRE)
-        ys[yy, xx] = part[:, :RY]
-        xs[xx, yy] = part[:, RY : RY + RX]
-        zs[:, yy, xx] = part[:, RY + RX :]
+        part = part.T.reshape(nz, RY + RX + RZ, cols)
+        for k, half in enumerate(split(part)):
+            ys[k, yy, xx] = half[:, :RY]
+            xs[k, xx, yy] = half[:, RY : RY + RX]
+            zs[k, :, yy, xx] = half[:, RY + RX :]
         if i == 0:
             pl.semaphore_wait(barrier, len(peers))
-        if dy:
-            send(ys.at[yy, xx], yr.at[xx], ysend.at[dx], yrecv.at[dx], ypeer)
-        if dx:
-            send(xs.at[xx, yy], xr.at[dx - 1, yy], xsend.at[dx - 1, dy], xrecv.at[dx - 1, dy], xpeers[dx - 1])
-    for d in range(1, nz):
-        send(zs.at[hop(z, d, nz)], zr.at[d - 1], zsend.at[d - 1], zrecv.at[d - 1], zpeers[d - 1])
+        first_sends(0, dy, dx)
+    last_sends(0)
     for d in range(1, nl):
         send(oh.at[g], oh.at[g], osend.at[d - 1], orecv.at[d - 1], lpeers[d - 1])
-
-    for dx in xorder:
-        xx = hop(x, dx, nx)
-        wait(yr.at[xx], yrecv.at[dx])
-        y2s[xx] = (ys[y, xx].astype(F32) + yr[xx].astype(F32)).astype(WIRE)
-        if dx:
-            send(y2s.at[xx], y2r.at[dx - 1], y2send.at[dx - 1], y2recv.at[dx - 1], xpeers[dx - 1])
-    for dy in (1, 0):
-        yy = hop(y, dy, ny)
-        acc = xs[x, yy].astype(F32)
+    for dy, dx in order:
+        first_sends(1, dy, dx)
+    last_sends(1)
+
+    def reduce1(k):
+        for dx in xorder:
+            xx = hop(x, dx, nx)
+            wait(yr.at[k, xx], yrecv.at[k, dx])
+            put(k, lambda j: y2s.at[j, xx], [ys[k, y, xx], yr[k, xx]])
+            if dx:
+                send(y2s.at[k, xx], y2r.at[k, dx - 1], y2send.at[k, dx - 1], y2recv.at[k, dx - 1], xpeers[dx - 1])
+        for dy in (1, 0):
+            yy = hop(y, dy, ny)
+            for d in range(1, nx):
+                wait(xr.at[k, d - 1, yy], xrecv.at[k, d - 1, dy])
+            put(k, lambda j: x2s.at[j, yy], [xs[k, x, yy]] + [xr[k, d - 1, yy] for d in range(1, nx)])
+            if dy:
+                send(x2s.at[k, yy], x2r.at[k], x2send.at[k], x2recv.at[k], ypeer)
+        for d in range(1, nz):
+            wait(zr.at[k, d - 1], zrecv.at[k, d - 1])
+        put(k, lambda j: z2s.at[j], [zs[k, z]] + [zr[k, d - 1] for d in range(1, nz)])
+        send(z2s.at[k, 1 - y], z2r.at[k], z2send.at[k], z2recv.at[k], ypeer)
+
+    def reduce2(k):
+        wait(x2r.at[k], x2recv.at[k])
+        put(k, lambda j: x3s.at[j], [x2s[k, y], x2r[k]])
+        for d in range(1, nz):
+            send(x3s.at[k, hop(z, d, nz)], x3r.at[k, d - 1], x3send.at[k, d - 1], x3recv.at[k, d - 1], zpeers[d - 1])
         for d in range(1, nx):
-            wait(xr.at[d - 1, yy], xrecv.at[d - 1, dy])
-            acc = acc + xr[d - 1, yy].astype(F32)
-        x2s[yy] = acc.astype(WIRE)
-        if dy:
-            send(x2s.at[yy], x2r, x2send, x2recv, ypeer)
-    acc = zs[z].astype(F32)
-    for d in range(1, nz):
-        wait(zr.at[d - 1], zrecv.at[d - 1])
-        acc = acc + zr[d - 1].astype(F32)
-    z2s[...] = acc.astype(WIRE)
-    send(z2s.at[1 - y], z2r, z2send, z2recv, ypeer)
-
-    wait(x2r, x2recv)
-    x3s[...] = (x2s[y].astype(F32) + x2r[...].astype(F32)).astype(WIRE)
-    for d in range(1, nz):
-        send(x3s.at[hop(z, d, nz)], x3r.at[d - 1], x3send.at[d - 1], x3recv.at[d - 1], zpeers[d - 1])
-    acc = y2s[x].astype(F32)
-    for d in range(1, nx):
-        wait(y2r.at[d - 1], y2recv.at[d - 1])
-        acc = acc + y2r[d - 1].astype(F32)
-    y3s[...] = acc.astype(WIRE)
-    for d in range(1, nz):
-        send(y3s.at[hop(z, d, nz)], y3r.at[d - 1], y3send.at[d - 1], y3recv.at[d - 1], zpeers[d - 1])
-    wait(z2r, z2recv)
-    z3s[...] = (z2s[y].astype(F32) + z2r[...].astype(F32)).astype(WIRE)
-    for d in range(1, nx):
-        send(z3s.at[hop(x, d, nx)], z3r.at[d - 1], z3send.at[d - 1], z3recv.at[d - 1], xpeers[d - 1])
+            wait(y2r.at[k, d - 1], y2recv.at[k, d - 1])
+        put(k, lambda j: y3s.at[j], [y2s[k, x]] + [y2r[k, d - 1] for d in range(1, nx)])
+        for d in range(1, nz):
+            send(y3s.at[k, hop(z, d, nz)], y3r.at[k, d - 1], y3send.at[k, d - 1], y3recv.at[k, d - 1], zpeers[d - 1])
+        wait(z2r.at[k], z2recv.at[k])
+        put(k, lambda j: z3s.at[j], [z2s[k, y], z2r[k]])
+        for d in range(1, nx):
+            send(z3s.at[k, hop(x, d, nx)], z3r.at[k, d - 1], z3send.at[k, d - 1], z3recv.at[k, d - 1], xpeers[d - 1])
 
     parts = ((0, RY), (RY, RX), (RY + RX, RZ))
 
-    def finish(own, r, rsem, n, part):
+    def finish(k, own, r, rsem, n, part):
         lo, size = parts[part]
-        acc = own.astype(F32)
         for d in range(1, n):
-            wait(r.at[d - 1], rsem.at[d - 1])
-            acc = acc + r[d - 1].astype(F32)
-        top = acc.astype(BF16)
-        high[g, lo : lo + size] = top
-        low[g, lo : lo + size] = (acc - top.astype(F32)).astype(BF16)
-        for d in range(1, nl):
-            ref = high.at[g, pl.ds(lo, size)]
-            send(ref, ref, gsend.at[part, d - 1], grecv.at[part, d - 1], lpeers[d - 1])
-
-    finish(x3s[z], x3r, x3recv, nz, 1)
-    finish(z3s[x], z3r, z3recv, nx, 2)
-    finish(y3s[z], y3r, y3recv, nz, 0)
-    for d in range(1, nl):
-        send(low.at[g], low.at[g], lsend.at[d - 1], lrecv.at[d - 1], lpeers[d - 1])
+            wait(r.at[k, d - 1], rsem.at[k, d - 1])
+        put(k, lambda j: both.at[j, g, pl.ds(lo, size)], [own] + [r[k, d - 1] for d in range(1, n)])
+        if k == 0:
+            for d in range(1, nl):
+                ref = both.at[0, g, pl.ds(lo, size)]
+                send(ref, ref, gsend.at[part, d - 1], grecv.at[part, d - 1], lpeers[d - 1])
+
+    def reduce3(k):
+        finish(k, x3s[k, z], x3r, x3recv, nz, 1)
+        finish(k, z3s[k, x], z3r, z3recv, nx, 2)
+        finish(k, y3s[k, z], y3r, y3recv, nz, 0)
+        if k == 1:
+            for d in range(1, nl):
+                send(both.at[1, g], both.at[1, g], lsend.at[d - 1], lrecv.at[d - 1], lpeers[d - 1])
+
+    for stage, k in ORDER:
+        (reduce1, reduce2, reduce3)[stage - 1](k)
 
     for d in range(1, nl):
         src = hop(g, nl - d, nl)
         wait(oh.at[src], orecv.at[d - 1])
         for part, (lo, size) in enumerate(parts):
-            wait(high.at[src, pl.ds(lo, size)], grecv.at[part, d - 1])
-
-    slots = high[...].astype(F32)
+            wait(both.at[0, src, pl.ds(lo, size)], grecv.at[part, d - 1])
+
+    slots = both[0].astype(F32)
     total = jnp.sum(slots, axis=0)
-    both = total + pltpu.roll(total, ranks, 1)
-    prods = jnp.sum(slots * both[None], axis=1)
+    twice = total + pltpu.roll(total, ranks, 1)
+    prods = jnp.sum(slots * twice[None], axis=1)
     first_slot = lane < ranks
     dot0 = jnp.sum(jnp.where(first_slot, prods, 0.0), axis=1, keepdims=True)
     dot1 = jnp.sum(jnp.where(first_slot, 0.0, prods), axis=1, keepdims=True)
-    square = jnp.sum(jnp.where(first_slot, jnp.sum(both * both, axis=0, keepdims=True), 0.0), axis=1, keepdims=True)
+    square = jnp.sum(jnp.where(first_slot, jnp.sum(twice * twice, axis=0, keepdims=True), 0.0), axis=1, keepdims=True)
     oh0, oh1 = oh[:, 0, :], oh[:, 1, :]
     vec = jnp.sum(oh0 * dot0 + oh1 * dot1, axis=0, keepdims=True)
     langs = old.shape[0]
@@ -211,8 +236,8 @@
     w1 = jnp.sum(oh1 * weights, axis=1, keepdims=True)
     slot_weight = jnp.where(first_slot, w0, w1)
     for d in range(1, nl):
-        wait(low.at[hop(g, nl - d, nl)], lrecv.at[d - 1])
-    slots = slots + low[...].astype(F32)
+        wait(both.at[1, hop(g, nl - d, nl)], lrecv.at[d - 1])
+    slots = slots + both[1].astype(F32)
     total = jnp.sum(slots * slot_weight[:, None, :], axis=0).T
     update[...] = total[:ranks] + total[ranks:]
 
@@ -242,7 +267,8 @@
     vmem = pl.BlockSpec(memory_space=pltpu.VMEM)
     smem = pl.BlockSpec(memory_space=pltpu.SMEM)
     dma = pltpu.SemaphoreType.DMA
-    b = lambda *s: pltpu.VMEM(s + (cols,), WIRE)
+    b = lambda *s: pltpu.VMEM((2,) + s + (cols,), BF16)
+    dma2 = lambda *s: dma((2,) + s)
     mat = jax.ShapeDtypeStruct((ranks, rows), F32)
     scratch = [
         pltpu.VMEM((ny * nx, 2, hidden.shape[1], blk), jnp.bfloat16),
@@ -252,15 +278,15 @@
         b(nx - 1, nz, RY), b(nz, RX), b(nx, RZ),
         b(nz, RY), b(nz, RX), b(nx, RZ),
         b(nz - 1, RY), b(nz - 1, RX), b(nx - 1, RZ),
-        pltpu.VMEM((nl, rows, cols), BF16), pltpu.VMEM((nl, rows, cols), BF16),
+        b(nl, rows),
         pltpu.VMEM((nl, 2, 128), F32),
         pltpu.VMEM((ny * nx * nz, 1, 128), F32),
         dma((ny * nx,)),
-        dma((nx,)), dma((nx,)), dma((nx - 1, ny)), dma((nx - 1, ny)), dma((nz - 1,)), dma((nz - 1,)),
-        dma((nx - 1,)), dma((nx - 1,)), dma, dma, dma, dma,
-        dma((nz - 1,)), dma((nz - 1,)), dma((nz - 1,)), dma((nz - 1,)), dma((nx - 1,)), dma((nx - 1,)),
-        dma((3, nl - 1)), dma((3, nl - 1)), dma((nl - 1,)), dma((nl - 1,)),
-        dma((nl - 1,)), dma((nl - 1,)), dma, dma,
+        dma2(nx), dma2(nx), dma2(nx - 1, ny), dma2(nx - 1, ny), dma2(nz - 1), dma2(nz - 1),
+        dma2(nx - 1), dma2(nx - 1), dma2(), dma2(), dma2(), dma2(),
+        dma2(nz - 1), dma2(nz - 1), dma2(nz - 1), dma2(nz - 1), dma2(nx - 1), dma2(nx - 1),
+        dma((3, nl - 1)), dma((3, nl - 1)), dma((nl - 1,)), dma((nl - 1,)), dma((nl - 1,)), dma((nl - 1,)),
+        dma, dma,
     ]
     update, logw = pl.pallas_call(
         functools.partial(kernel, nl, ny, nx, nz),

time: 58.2 us -> 56.1 us (0.964)
  Pallas kernels: 57.3 us -> 55.2 us
    pallas_call x1, Pallas kernels: 55.9 us -> 53.7 us  [local(): pl.pallas_call(functools.partial(kernel, nl, ny, nx, nz), out_shape=(mat,...]
where the time goes in v3:
time: 56.1 us; the launch traced here: 55.8 us
  Pallas kernels  55.2 us (98%)
  between operations  0.64 us (1%)
    pallas_call x1, Pallas kernels, local(): pl.pallas_call(functools.partial(kernel, nl, ny, nx, nz), out_shape=(mat,...  53.7 us
    pallas_call x1, Pallas kernels, local(): pl.pallas_call(adamw, out_shape=(mat, mat, mat, jax.ShapeDtypeStruct(old_...  1.47 us

profile of v3, /device:TPU:1, one launch (start us, length us, event | category | flops | bytes accessed | tf_op | source)
XLA Modules:
  0.0 55.8 jit_solution(180307032844020847)
XLA Ops:
  0.6 53.7 %reweight.1 = (f32[64,80]{1,0:T(8,128)}, f32[1,128]{1,0:T(1,128)}) custom-call(bf16[2,128,5120]{2,1,0:T(8,128)(2,1)} %hid.1, bf16[2,64,128]{2,1,0:T(8,128)(2,1)} %bitcast.7, s32[2]{0:T(128)} %ids.1, f32[16]{0:T(128)} %old.1), custom_call_target="tpu_custom_call" | custom-call | tf_op jit(solution)/shard_map/reweight/pallas_call | solution.py:291
  54.4 1.5 %adamw.1 = (f32[64,80]{1,0:T(8,128)}, f32[64,80]{1,0:T(8,128)}, f32[64,80]{1,0:T(8,128)}, f32[16]{0:T(128)}) custom-call(f32[64,80]{1,0:T(8,128)} %get-tuple-element.10.grad, f32[1,128]{1,0:T(1,128)} %get-tuple-element.11.logw, f32[64,80]{1,0:T(8,128)} %bitcast.8, f32[64,80]{1,0:T(8,128)} %bitcast.9, f32[64,80]{1,0:T(8,128)} %bitcast.10), custom_call_target="tpu_custom_call" | custom-call | tf_op jit(solution)/shard_map/adamw/pallas_call | solution.py:302

commit v4 on v3

--- a/solution.py
+++ b/solution.py
@@ -12,7 +12,11 @@
 RY, RX, RZ = 32, 32, 16
 F32 = jnp.float32
 BF16 = jnp.bfloat16
-ORDER = ((1, 0), (2, 0), (1, 1), (3, 0), (2, 1), (3, 1))
+ORDER = (
+    "y10", "lx", "x10", "z10", "x20", "y20", "z20", "y11", "z11", "x11", "x30", "z30", "y30",
+    "x21", "y21", "z21",
+)
+LATE = ("x31", "z31", "y31")
 
 
 def kernel(
@@ -24,7 +28,7 @@
     hsem, ysend, yrecv, xsend, xrecv, zsend, zrecv,
     y2send, y2recv, x2send, x2recv, z2send, z2recv,
     y3send, y3recv, x3send, x3recv, z3send, z3recv,
-    gsend, grecv, lsend, lrecv, osend, orecv, asend, arecv,
+    gsend, grecv, fsend, frecv, osend, orecv, asend, arecv,
 ):
     g = lax.axis_index("language")
     f = lax.axis_index("fsdp")
@@ -48,7 +52,8 @@
     zpeers = [at(y, x, hop(z, d, nz)) for d in range(1, nz)]
     xpeers = [at(y, hop(x, d, nx), z) for d in range(1, nx)]
     ypeer = at(1 - y, x, z)
-    lpeers = [lang(hop(g, d, nl)) for d in range(1, nl)]
+    twin = g + 1 - 2 * (g % 2)
+    lpeers = [lang(twin)] + [lang(hop(g, 2 * d, nl)) for d in range(1, nl // 2)]
     peers = [ypeer] + xpeers + zpeers + lpeers
 
     barrier = pltpu.get_barrier_semaphore()
@@ -107,11 +112,11 @@
         else:
             dst(1)[...] = (total + dst(1)[...].astype(F32)).astype(BF16)
 
-    def first_sends(k, dy, dx):
+    def first_sends(k, dy, dx, do_y=True, do_x=True):
         yy, xx = hop(y, dy, ny), hop(x, dx, nx)
-        if dy:
+        if dy and do_y:
             send(ys.at[k, yy, xx], yr.at[k, xx], ysend.at[k, dx], yrecv.at[k, dx], ypeer)
-        if dx:
+        if dx and do_x:
             send(
                 xs.at[k, xx, yy], xr.at[k, dx - 1, yy], xsend.at[k, dx - 1, dy], xrecv.at[k, dx - 1, dy],
                 xpeers[dx - 1],
@@ -135,19 +140,21 @@
             pl.semaphore_wait(barrier, len(peers))
         first_sends(0, dy, dx)
     last_sends(0)
-    for d in range(1, nl):
-        send(oh.at[g], oh.at[g], osend.at[d - 1], orecv.at[d - 1], lpeers[d - 1])
+    for d, p in enumerate(lpeers):
+        send(oh.at[g], oh.at[g], osend.at[d], orecv.at[d], p)
+    last_sends(1)
     for dy, dx in order:
-        first_sends(1, dy, dx)
-    last_sends(1)
-
-    def reduce1(k):
+        first_sends(1, dy, dx, do_x=False)
+
+    def first_y(k):
         for dx in xorder:
             xx = hop(x, dx, nx)
             wait(yr.at[k, xx], yrecv.at[k, dx])
             put(k, lambda j: y2s.at[j, xx], [ys[k, y, xx], yr[k, xx]])
             if dx:
                 send(y2s.at[k, xx], y2r.at[k, dx - 1], y2send.at[k, dx - 1], y2recv.at[k, dx - 1], xpeers[dx - 1])
+
+    def first_x(k):
         for dy in (1, 0):
             yy = hop(y, dy, ny)
             for d in range(1, nx):
@@ -155,54 +162,89 @@
             put(k, lambda j: x2s.at[j, yy], [xs[k, x, yy]] + [xr[k, d - 1, yy] for d in range(1, nx)])
             if dy:
                 send(x2s.at[k, yy], x2r.at[k], x2send.at[k], x2recv.at[k], ypeer)
+
+    def first_z(k):
         for d in range(1, nz):
             wait(zr.at[k, d - 1], zrecv.at[k, d - 1])
         put(k, lambda j: z2s.at[j], [zs[k, z]] + [zr[k, d - 1] for d in range(1, nz)])
         send(z2s.at[k, 1 - y], z2r.at[k], z2send.at[k], z2recv.at[k], ypeer)
 
-    def reduce2(k):
+    def second_x(k):
         wait(x2r.at[k], x2recv.at[k])
         put(k, lambda j: x3s.at[j], [x2s[k, y], x2r[k]])
         for d in range(1, nz):
             send(x3s.at[k, hop(z, d, nz)], x3r.at[k, d - 1], x3send.at[k, d - 1], x3recv.at[k, d - 1], zpeers[d - 1])
+
+    def second_y(k):
         for d in range(1, nx):
             wait(y2r.at[k, d - 1], y2recv.at[k, d - 1])
         put(k, lambda j: y3s.at[j], [y2s[k, x]] + [y2r[k, d - 1] for d in range(1, nx)])
         for d in range(1, nz):
             send(y3s.at[k, hop(z, d, nz)], y3r.at[k, d - 1], y3send.at[k, d - 1], y3recv.at[k, d - 1], zpeers[d - 1])
+
+    def second_z(k):
         wait(z2r.at[k], z2recv.at[k])
         put(k, lambda j: z3s.at[j], [z2s[k, y], z2r[k]])
         for d in range(1, nx):
             send(z3s.at[k, hop(x, d, nx)], z3r.at[k, d - 1], z3send.at[k, d - 1], z3recv.at[k, d - 1], xpeers[d - 1])
 
     parts = ((0, RY), (RY, RX), (RY + RX, RZ))
-
-    def finish(k, own, r, rsem, n, part):
+    chips = nl // 2
+
+    def third(k, own, r, rsem, n, part):
         lo, size = parts[part]
         for d in range(1, n):
             wait(r.at[k, d - 1], rsem.at[k, d - 1])
         put(k, lambda j: both.at[j, g, pl.ds(lo, size)], [own] + [r[k, d - 1] for d in range(1, n)])
+        ref = both.at[k, g, pl.ds(lo, size)]
+        for d, p in enumerate(lpeers):
+            send(ref, ref, gsend.at[k, part, d], grecv.at[k, part, d], p)
+
+    def third_x(k):
+        third(k, x3s[k, z], x3r, x3recv, nz, 1)
+
+    def third_z(k):
+        third(k, z3s[k, x], z3r, z3recv, nx, 2)
+
+    def third_y(k):
+        third(k, y3s[k, z], y3r, y3recv, nz, 0)
+
+    def low_x(k):
+        for dy, dx in order:
+            first_sends(1, dy, dx, do_y=False)
+
+    def hand_over(k):
+        for d in range(1, chips):
+            src = hop(g, nl - 2 * d, nl)
+            for part, (lo, size) in enumerate(parts):
+                wait(both.at[k, src, pl.ds(lo, size)], grecv.at[k, part, d])
+            send(both.at[k, src], both.at[k, src], fsend.at[k, d - 1], frecv.at[k, d - 1], lpeers[0])
+            if k == 0:
+                wait(oh.at[src], orecv.at[d])
+                send(oh.at[src], oh.at[src], osend.at[chips + d - 1], orecv.at[chips + d - 1], lpeers[0])
+
+    def take_over(k):
+        for part, (lo, size) in enumerate(parts):
+            wait(both.at[k, twin, pl.ds(lo, size)], grecv.at[k, part, 0])
         if k == 0:
-            for d in range(1, nl):
-                ref = both.at[0, g, pl.ds(lo, size)]
-                send(ref, ref, gsend.at[part, d - 1], grecv.at[part, d - 1], lpeers[d - 1])
-
-    def reduce3(k):
-        finish(k, x3s[k, z], x3r, x3recv, nz, 1)
-        finish(k, z3s[k, x], z3r, z3recv, nx, 2)
-        finish(k, y3s[k, z], y3r, y3recv, nz, 0)
-        if k == 1:
-            for d in range(1, nl):
-                send(both.at[1, g], both.at[1, g], lsend.at[d - 1], lrecv.at[d - 1], lpeers[d - 1])
-
-    for stage, k in ORDER:
-        (reduce1, reduce2, reduce3)[stage - 1](k)
-
-    for d in range(1, nl):
-        src = hop(g, nl - d, nl)
-        wait(oh.at[src], orecv.at[d - 1])
-        for part, (lo, size) in enumerate(parts):
-            wait(both.at[0, src, pl.ds(lo, size)], grecv.at[part, d - 1])
+            wait(oh.at[twin], orecv.at[0])
+        for d in range(1, chips):
+            src = hop(twin, nl - 2 * d, nl)
+            wait(both.at[k, src], frecv.at[k, d - 1])
+            if k == 0:
+                wait(oh.at[src], orecv.at[chips + d - 1])
+
+    steps = dict(
+        y1=first_y, x1=first_x, z1=first_z, x2=second_x, y2=second_y, z2=second_z,
+        x3=third_x, y3=third_y, z3=third_z, lx=low_x,
+    )
+    for step in ORDER:
+        steps[step[:2]](int(step[2:] or 0))
+
+    hand_over(0)
+    for step in LATE:
+        steps[step[:2]](int(step[2:] or 0))
+    take_over(0)
 
     slots = both[0].astype(F32)
     total = jnp.sum(slots, axis=0)
@@ -219,9 +261,15 @@
 
     ar[f] = vec
     n = ny * nx * nz
-    for d in range(1, n):
+
+    def far(d):
+        dy, dx, dz = d // (nx * nz), d // nz % nx, d % nz
+        return dy + min(dx, nx - dx) + min(dz, nz - dz)
+
+    for d in sorted(range(1, n), key=lambda d: -far(d)):
         yy, xx, zz = hop(y, d // (nx * nz), ny), hop(x, d // nz % nx, nx), hop(z, d % nz, nz)
         send(ar.at[f], ar.at[f], asend, arecv, at(yy, xx, zz), False)
+    hand_over(1)
     wait(ar.at[pl.ds(0, n - 1)], arecv)
     vec = jnp.sum(ar[...], axis=0)
 
@@ -235,8 +283,7 @@
     w0 = jnp.sum(oh0 * weights, axis=1, keepdims=True)
     w1 = jnp.sum(oh1 * weights, axis=1, keepdims=True)
     slot_weight = jnp.where(first_slot, w0, w1)
-    for d in range(1, nl):
-        wait(both.at[1, hop(g, nl - d, nl)], lrecv.at[d - 1])
+    take_over(1)
     slots = slots + both[1].astype(F32)
     total = jnp.sum(slots * slot_weight[:, None, :], axis=0).T
     update[...] = total[:ranks] + total[ranks:]
@@ -285,7 +332,7 @@
         dma2(nx), dma2(nx), dma2(nx - 1, ny), dma2(nx - 1, ny), dma2(nz - 1), dma2(nz - 1),
         dma2(nx - 1), dma2(nx - 1), dma2(), dma2(), dma2(), dma2(),
         dma2(nz - 1), dma2(nz - 1), dma2(nz - 1), dma2(nz - 1), dma2(nx - 1), dma2(nx - 1),
-        dma((3, nl - 1)), dma((3, nl - 1)), dma((nl - 1,)), dma((nl - 1,)), dma((nl - 1,)), dma((nl - 1,)),
+        dma2(3, nl // 2), dma2(3, nl // 2), dma2(max(nl // 2 - 1, 1)), dma2(max(nl // 2 - 1, 1)), dma((nl - 1,)), dma((nl - 1,)),
         dma, dma,
     ]
     update, logw = pl.pallas_call(

time: 56.1 us -> 53.2 us (0.948)
  Pallas kernels: 55.2 us -> 52.2 us
    pallas_call x1, Pallas kernels: 53.7 us -> 50.8 us  [local(): pl.pallas_call(functools.partial(kernel, nl, ny, nx, nz), out_shape=(mat,...]
where the time goes in v4:
time: 53.2 us; the launch traced here: 52.9 us
  Pallas kernels  52.2 us (98%)
  between operations  0.64 us (1%)
    pallas_call x1, Pallas kernels, local(): pl.pallas_call(functools.partial(kernel, nl, ny, nx, nz), out_shape=(mat,...  50.8 us
    pallas_call x1, Pallas kernels, local(): pl.pallas_call(adamw, out_shape=(mat, mat, mat, jax.ShapeDtypeStruct(old_...  1.47 us

profile of v4, /device:TPU:1, one launch (start us, length us, event | category | flops | bytes accessed | tf_op | source)
XLA Modules:
  0.0 52.9 jit_solution(17634836201223875806)
XLA Ops:
  0.6 50.8 %reweight.1 = (f32[64,80]{1,0:T(8,128)}, f32[1,128]{1,0:T(1,128)}) custom-call(bf16[2,128,5120]{2,1,0:T(8,128)(2,1)} %hid.1, bf16[2,64,128]{2,1,0:T(8,128)(2,1)} %bitcast.7, s32[2]{0:T(128)} %ids.1, f32[16]{0:T(128)} %old.1), custom_call_target="tpu_custom_call" | custom-call | tf_op jit(solution)/shard_map/reweight/pallas_call | solution.py:338
  51.4 1.5 %adamw.1 = (f32[64,80]{1,0:T(8,128)}, f32[64,80]{1,0:T(8,128)}, f32[64,80]{1,0:T(8,128)}, f32[16]{0:T(128)}) custom-call(f32[64,80]{1,0:T(8,128)} %get-tuple-element.10.grad, f32[1,128]{1,0:T(1,128)} %get-tuple-element.11.logw, f32[64,80]{1,0:T(8,128)} %bitcast.8, f32[64,80]{1,0:T(8,128)} %bitcast.9, f32[64,80]{1,0:T(8,128)} %bitcast.10), custom_call_target="tpu_custom_call" | custom-call | tf_op jit(solution)/shard_map/adamw/pallas_call | solution.py:349

commit v5 on v4

--- a/solution.py
+++ b/solution.py
@@ -241,6 +241,7 @@
     for step in ORDER:
         steps[step[:2]](int(step[2:] or 0))
 
+    early = len(sent)
     hand_over(0)
     for step in LATE:
         steps[step[:2]](int(step[2:] or 0))
@@ -269,6 +270,8 @@
     for d in sorted(range(1, n), key=lambda d: -far(d)):
         yy, xx, zz = hop(y, d // (nx * nz), ny), hop(x, d // nz % nx, nx), hop(z, d % nz, nz)
         send(ar.at[f], ar.at[f], asend, arecv, at(yy, xx, zz), False)
+    for c in sent[:early]:
+        c.wait_send()
     hand_over(1)
     wait(ar.at[pl.ds(0, n - 1)], arecv)
     vec = jnp.sum(ar[...], axis=0)
@@ -288,7 +291,7 @@
     total = jnp.sum(slots * slot_weight[:, None, :], axis=0).T
     update[...] = total[:ranks] + total[ranks:]
 
-    for c in sent:
+    for c in sent[early:]:
         c.wait_send()
     pltpu.make_async_copy(ar.at[pl.ds(0, n - 1)], ar.at[pl.ds(0, n - 1)], asend).wait()
 

time: 53.2 us -> 53 us (level)
  no operation moved by 1% of the time
where the time goes in v5:
time: 53 us; the launch traced here: 52.7 us
  Pallas kernels  52.1 us (98%)
  between operations  0.64 us (1%)
    pallas_call x1, Pallas kernels, local(): pl.pallas_call(functools.partial(kernel, nl, ny, nx, nz), out_shape=(mat,...  50.6 us
    pallas_call x1, Pallas kernels, local(): pl.pallas_call(adamw, out_shape=(mat, mat, mat, jax.ShapeDtypeStruct(old_...  1.47 us

profile of v5, /device:TPU:1, one launch (start us, length us, event | category | flops | bytes accessed | tf_op | source)
XLA Modules:
  0.0 52.7 jit_solution(3634039222320804919)
XLA Ops:
  0.6 50.6 %reweight.1 = (f32[64,80]{1,0:T(8,128)}, f32[1,128]{1,0:T(1,128)}) custom-call(bf16[2,128,5120]{2,1,0:T(8,128)(2,1)} %hid.1, bf16[2,64,128]{2,1,0:T(8,128)(2,1)} %bitcast.7, s32[2]{0:T(128)} %ids.1, f32[16]{0:T(128)} %old.1), custom_call_target="tpu_custom_call" | custom-call | tf_op jit(solution)/shard_map/reweight/pallas_call | solution.py:341
  51.3 1.5 %adamw.1 = (f32[64,80]{1,0:T(8,128)}, f32[64,80]{1,0:T(8,128)}, f32[64,80]{1,0:T(8,128)}, f32[16]{0:T(128)}) custom-call(f32[64,80]{1,0:T(8,128)} %get-tuple-element.10.grad, f32[1,128]{1,0:T(1,128)} %get-tuple-element.11.logw, f32[64,80]{1,0:T(8,128)} %bitcast.8, f32[64,80]{1,0:T(8,128)} %bitcast.9, f32[64,80]{1,0:T(8,128)} %bitcast.10), custom_call_target="tpu_custom_call" | custom-call | tf_op jit(solution)/shard_map/adamw/pallas_call | solution.py:352
